TPU v7x, 256 devices: a whole 4x4x8 slice. The times are simulated.
256 devices in a mesh: blk: 64 (over y_lo, z, x), row: 4 (over y_hi, core).
Axes of the slice: x: 4, y: 4 (y_hi: 2, y_lo: 2; y = y_hi * 2 + y_lo), z: 8, core: 2. Of those that a mesh axis runs over, the one named last changes fastest.
Arguments:
- transmission: float32 [16384, 2, 8192], P(('blk', 'row')), may hold values from -64 to 64, as said below
- assignment: int32 [256], replicated, may hold values from 0 to 255, each once
- pairing: int32 [2, 64], replicated, may hold values from 0 to 2
Outputs:
- rotated: float32 [16384, 2, 8192], P(('blk', 'row'))
Inputs may be any that keep to these rules, and one draw needn't show every extreme that they name: `transmission`: entries are real and imaginary parts of a measured speckle field; columns and rows have differing gains. `assignment`: A permutation of the block numbers.
All inputs are finite; a program needn't handle non-finite values.
Results may differ from a plain program's by a relative error of at most 0.00016.
Values sent between devices are 32-bit elements; how exact they have to be, the bound alone decides.
A program may use at most 128 MiB of HBM per device.

v0:
```python
import jax
import jax.numpy as jnp
from jax import lax
from jax.sharding import PartitionSpec as P

ROWS = 16384
BLOCK = 32
SLOTS = 4
ROUNDS = 2
NS_STEPS = 6


def shifted(block, axis, distance):
    devices = range(lax.axis_size(axis))
    route = [((i - distance) % len(devices), i) for i in devices]
    return lax.ppermute(block, axis, route)


def kernel_rotation(real_part, imag_part):
    kernel = jnp.concatenate(
        [
            jnp.concatenate([real_part, imag_part], axis=1),
            jnp.concatenate([-imag_part, real_part], axis=1),
        ],
        axis=0,
    )
    scale = jnp.sqrt(jnp.sum(kernel * kernel))
    eye = jnp.eye(kernel.shape[0], dtype=jnp.float32)
    upper = kernel / scale
    lower = eye
    for step in range(NS_STEPS):
        middle = 1.5 * eye - 0.5 * jnp.dot(lower, upper, precision=lax.Precision.HIGHEST)
        upper = jnp.dot(upper, middle, precision=lax.Precision.HIGHEST)
        lower = jnp.dot(middle, lower, precision=lax.Precision.HIGHEST)
    return lower * jnp.sqrt(ROWS / scale)


def pair_rotation(gram):
    half = gram.shape[0] // 2
    real_part = gram[:half, :half] + gram[half:, half:]
    imag_part = gram[:half, half:] - gram[half:, :half]
    return kernel_rotation(real_part, imag_part)


def local_gram(joined):
    return jnp.dot(joined.T, joined, precision=lax.Precision.HIGHEST)


def summed_pair(joined):
    gram = lax.psum(local_gram(joined), "row")
    return jnp.dot(joined, pair_rotation(gram), precision=lax.Precision.HIGHEST)


def column_index(held, total_cols):
    parts = jnp.arange(2, dtype=jnp.int32)[None, :, None, None] * total_cols
    starts = held[:, None, :, None] * BLOCK
    within = jnp.arange(BLOCK, dtype=jnp.int32)[None, None, None, :]
    return (parts + starts + within).reshape(-1)


def slot_columns(slots):
    parts = jnp.arange(2, dtype=jnp.int32)[:, None, None] * (SLOTS * BLOCK)
    starts = slots[None, :, None] * BLOCK
    within = jnp.arange(BLOCK, dtype=jnp.int32)[None, None, :]
    return (parts + starts + within).reshape(-1)


def inverse_of(index):
    return (
        jnp.zeros(index.shape, jnp.int32).at[index].set(jnp.arange(index.shape[0], dtype=jnp.int32))
    )


def turn_held(held):
    return jnp.stack(
        [held[:, 0], jnp.roll(held[:, 1], 1), jnp.roll(held[:, 2], -1), held[:, 3]], axis=1
    )


def on_device(transmission, assignment, pairing):
    nblk = lax.axis_size("blk")
    me_blk = lax.axis_index("blk")
    row_part = transmission.shape[0]
    total_cols = transmission.shape[2]
    orders = jnp.array([[0, 1, 2, 3], [0, 2, 1, 3], [0, 3, 1, 2]], dtype=jnp.int32)
    held = assignment.reshape(nblk, SLOTS)
    flat = transmission.reshape(row_part, 2 * total_cols)
    outgoing = jnp.take(flat, column_index(held, total_cols), axis=1)
    blocks = lax.all_to_all(outgoing, "blk", split_axis=1, concat_axis=0, tiled=True)
    owned_rows = blocks.shape[0]
    for rnd in range(ROUNDS):
        pick = pairing[rnd, me_blk]
        order = orders[pick]
        first_cols = slot_columns(order[0:2])
        second_cols = slot_columns(order[2:4])
        first = jnp.take(blocks, first_cols, axis=1)
        second = jnp.take(blocks, second_cols, axis=1)
        new_first = summed_pair(first)
        new_second = summed_pair(second)
        joined = jnp.concatenate([new_first, new_second], axis=1)
        back = inverse_of(jnp.concatenate([first_cols, second_cols]))
        blocks = jnp.take(joined, back, axis=1)
        if rnd < ROUNDS - 1:
            lanes = owned_rows * 2 * BLOCK // 128
            up_cols = slot_columns(jnp.array([1], dtype=jnp.int32))
            down_cols = slot_columns(jnp.array([2], dtype=jnp.int32))
            moved_up = shifted(jnp.take(blocks, up_cols, axis=1).reshape(lanes, 128), "blk", 1)
            moved_down = shifted(jnp.take(blocks, down_cols, axis=1).reshape(lanes, 128), "blk", -1)
            blocks = blocks.at[:, up_cols].set(moved_up.reshape(owned_rows, 2 * BLOCK))
            blocks = blocks.at[:, down_cols].set(moved_down.reshape(owned_rows, 2 * BLOCK))
            held = turn_held(held)
    returned = lax.all_to_all(blocks, "blk", split_axis=0, concat_axis=1, tiled=True)
    placed = column_index(held, total_cols)
    rotated = jnp.take(returned, inverse_of(placed), axis=1)
    return rotated.reshape(row_part, 2, total_cols)


def solution(mesh):
    placed = (P(("blk", "row"), None, None), P(), P())
    return jax.shard_map(
        on_device,
        mesh=mesh,
        in_specs=placed,
        out_specs=P(("blk", "row"), None, None),
        check_vma=False,
    )
```

profile of v0, /device:TPU:6, one launch (start us, length us, event | category | flops | bytes accessed | tf_op | source)
XLA Modules:
  0.0 666.9 jit_solution(6179644993815325899)
XLA Ops:
  10.4 8.4 %copy.43 = f32[64,2,8192]{0,2,1:T(8,128)} copy(f32[64,2,8192]{2,1,0:T(2,128)} %param.14) | data formatting | bytes 8388608 | tf_op args[0]
  18.8 58.2 %gather_fusion = f32[16384,64]{1,0:T(8,128)} fusion(f32[64,16384]{0,1:T(8,128)} %bitcast.203, s32[16384]{0:T(1024)S(1)} %fusion.68), kind=kCustom, calls=%fused_computation.clone | custom fusion | bytes 8454144 | tf_op jit(solution)/shard_map/jit(_take)/gather | solution.py:88
  77.0 13.1 %broadcast_select_fusion.1 = f32[16384,64]{1,0:T(8,128)} fusion(f32[16384,64]{1,0:T(8,128)} %gather_fusion, pred[16384]{0:T(1024)(128)(4,1)S(1)} %compare_and_fusion.1), kind=kLoop, calls=%fused_computation.20 | loop fusion | flops 1048576 | bytes 8404992 | tf_op jit(solution)/shard_map/jit(_take)/select_n | solution.py:88
  90.1 6.8 %copy.44 = f32[64,64,256]{2,0,1:T(8,128)} copy(f32[64,64,256]{0,2,1:T(8,128)} %bitcast.204) | data formatting | bytes 8388608 | tf_op jit(solution)/shard_map/all_to_all | solution.py:89
  96.9 13.3 %all-to-all-start = ((f32[64,64,256]{2,0,1:T(8,128)}), f32[64,64,256]{2,0,1:T(8,128)}, u32[]{:S(2)}, u32[]{:S(2)}) async-start(f32[64,64,256]{2,0,1:T(8,128)} %copy.44), calls=%async_computation | async-start | bytes 8388608 | tf_op jit(solution)/shard_map/all_to_all | solution.py:89
  117.8 87.9 %all-to-all-done = f32[64,64,256]{2,0,1:T(8,128)} async-done(((f32[64,64,256]{2,0,1:T(8,128)}), f32[64,64,256]{2,0,1:T(8,128)}, u32[]{:S(2)}, u32[]{:S(2)}) %all-to-all-start) | async-done | bytes 4194336 | tf_op jit(solution)/shard_map/all_to_all | solution.py:89
  205.7 5.6 copy.45
  211.3 5.6 gather_fusion.2
  231.0 40.0 %all-reduce.7.cloned.1.call-done = (f32[128,128]{1,0:T(8,128)}, f32[128,128]{1,0:T(8,128)}) async-done(((f32[128,128]{1,0:T(8,128)}, f32[128,128]{1,0:T(8,128)}), (f32[128,128]{1,0:T(8,128)}, f32[128,128]{1,0:T(8,128)})) %all-reduce.7.cloned.1.call-update) | async-done | bytes 131088 | tf_op jit(solution)/shard_map/psum | solution.py:50
  292.1 7.8 %gather_fusion.3 = f32[256,4096]{1,0:T(8,128)} fusion(f32[4096,256]{0,1:T(8,128)} %pad_maximum_fusion, s32[1024]{0:T(1024)S(1)} %pad_clamp_fusion.5), kind=kCustom, calls=%fused_computation.2.clone | custom fusion | bytes 8389632 | tf_op jit(solution)/shard_map/jit(_take)/gather | solution.py:102
  320.7 21.5 %collective-permute-done = f32[2048,128]{1,0:T(8,128)} collective-permute-done((f32[2048,128]{1,0:T(8,128)}, f32[2048,128]{1,0:T(8,128)}, u32[]{:S(2)}, u32[]{:S(2)}) %collective-permute-start) | collective-permute-done | bytes 1048608 | tf_op jit(solution)/shard_map/ppermute | solution.py:16
  352.6 5.3 scatter_fusion
  357.9 5.5 scatter_fusion.1
  363.4 5.6 gather_fusion.7
  381.1 44.9 %all-reduce.5.cloned.1.call-done = (f32[128,128]{1,0:T(8,128)}, f32[128,128]{1,0:T(8,128)}) async-done(((f32[128,128]{1,0:T(8,128)}, f32[128,128]{1,0:T(8,128)}), (f32[128,128]{1,0:T(8,128)}, f32[128,128]{1,0:T(8,128)})) %all-reduce.5.cloned.1.call-update) | async-done | bytes 131088 | tf_op jit(solution)/shard_map/psum | solution.py:50
  447.3 7.8 %gather_fusion.8 = f32[256,4096]{1,0:T(8,128)} fusion(f32[4096,256]{0,1:T(8,128)} %pad_maximum_fusion.1, s32[1024]{0:T(1024)S(1)} %pad_clamp_fusion), kind=kCustom, calls=%fused_computation.8.clone | custom fusion | bytes 8389632 | tf_op jit(solution)/shard_map/jit(_take)/gather | solution.py:102
  459.9 5.6 copy.51
  465.5 10.7 %all-to-all-start.1 = ((f32[64,64,256]{2,1,0:T(8,128)}), f32[64,64,256]{2,1,0:T(8,128)}, u32[]{:S(2)}, u32[]{:S(2)}) async-start(f32[64,64,256]{2,1,0:T(8,128)} %bitcast.206), calls=%async_computation.1 | async-start | bytes 8388608 | tf_op jit(solution)/shard_map/all_to_all | solution.py:112
  476.8 60.3 %scatter_custom_fusion.4 = s32[16384]{0:T(1024)S(1)} fusion(s32[16384]{0:T(1024)S(1)} %bitcast.209, s32[16384]{0:T(1024)S(1)} %iota.215, s32[]{:T(128)} %constant.15.clone.1), kind=kCustom, calls=%fused_computation.148 | custom fusion | bytes 65540 | tf_op jit(solution)/shard_map/scatter | solution.py:70
  537.2 35.8 %all-to-all-done.1 = f32[64,64,256]{2,1,0:T(8,128)} async-done(((f32[64,64,256]{2,1,0:T(8,128)}), f32[64,64,256]{2,1,0:T(8,128)}, u32[]{:S(2)}, u32[]{:S(2)}) %all-to-all-start.1) | async-done | bytes 4194336 | tf_op jit(solution)/shard_map/all_to_all | solution.py:112
  573.0 6.9 %copy.52 = f32[64,64,256]{0,2,1:T(8,128)} copy(f32[64,64,256]{2,0,1:T(8,128)} %bitcast.32) | data formatting | bytes 8388608 | tf_op jit(solution)/shard_map/all_to_all | solution.py:112
  579.9 58.2 %gather_fusion.9 = f32[16384,64]{1,0:T(8,128)} fusion(f32[64,16384]{0,1:T(8,128)} %bitcast.202, s32[16384]{0:T(1024)S(1)} %fusion.69), kind=kCustom, calls=%fused_computation.4.clone | custom fusion | bytes 8454144 | tf_op jit(solution)/shard_map/jit(_take)/gather | solution.py:114
  638.1 13.1 %broadcast_select_fusion = f32[16384,64]{1,0:T(8,128)} fusion(f32[16384,64]{1,0:T(8,128)} %gather_fusion.9, pred[16384]{0:T(1024)(128)(4,1)S(1)} %compare_and_fusion), kind=kLoop, calls=%fused_computation.19 | loop fusion | flops 1048576 | bytes 8404992 | tf_op jit(solution)/shard_map/jit(_take)/select_n | solution.py:114
  651.2 8.6 %copy.53 = f32[64,2,8192]{2,1,0:T(2,128)} copy(f32[64,2,8192]{0,2,1:T(8,128)} %bitcast.205) | data formatting | bytes 8388608 | tf_op jit(solution)/shard_map/reshape | solution.py:115
  (199 shorter events, 108.7 us)
Async XLA Ops:
  96.9 13.4 %copy-start.4 = (s32[2,64]{1,0:T(2,128)S(1)}, s32[2,64]{1,0:T(2,128)}, u32[]{:S(2)}) copy-start(s32[2,64]{1,0:T(2,128)} %param.16) | copy-start | bytes 1540
  96.9 17.8 %copy-start.5 = (s32[3,4]{1,0:T(4,128)S(1)}, s32[3,4]{1,0:T(4,128)}, u32[]{:S(2)}) copy-start(s32[3,4]{1,0:T(4,128)} %constant.22.clone) | copy-start | bytes 148
  96.9 108.8 %all-to-all-start = ((f32[64,64,256]{2,0,1:T(8,128)}), f32[64,64,256]{2,0,1:T(8,128)}, u32[]{:S(2)}, u32[]{:S(2)}) async-start(f32[64,64,256]{2,0,1:T(8,128)} %copy.44), calls=%async_computation | async-start | bytes 8388608 | tf_op jit(solution)/shard_map/all_to_all | solution.py:89
  110.2 160.8 %all-reduce.7.cloned.1.call-start = ((), (), s32[]{:S(2)}) async-start(), calls=%async_computation.3 | async-start | bytes 262144 | tf_op jit(solution)/shard_map/psum | solution.py:50
  228.9 197.0 %all-reduce.5.cloned.1.call-start = ((), (), s32[]{:S(2)}) async-start(), calls=%async_computation.2 | async-start | bytes 262144 | tf_op jit(solution)/shard_map/psum | solution.py:50
  271.0 5.6 copy-start.2
  287.4 2.2 copy-start
  316.6 25.7 %collective-permute-start = (f32[2048,128]{1,0:T(8,128)}, f32[2048,128]{1,0:T(8,128)}, u32[]{:S(2)}, u32[]{:S(2)}) collective-permute-start(f32[2048,128]{1,0:T(8,128)} %reshape.609), channel_id=1, source_target_pairs={{252,0},{0,4},{4,8},{8,12},{12,16},{16,20},{20,24},{24,28},{28,32}... | collective-permute-start | bytes 3145736 | tf_op jit(solution)/shard_map/ppermute | solution.py:16
  320.2 27.5 %collective-permute-start.1 = (f32[2048,128]{1,0:T(8,128)}, f32[2048,128]{1,0:T(8,128)}, u32[]{:S(2)}, u32[]{:S(2)}) collective-permute-start(f32[2048,128]{1,0:T(8,128)} %reshape.611), channel_id=1, source_target_pairs={{4,0},{8,4},{12,8},{16,12},{20,16},{24,20},{28,24},{32,28},{36,32}... | collective-permute-start | bytes 3145736 | tf_op jit(solution)/shard_map/ppermute | solution.py:16
  425.9 5.6 copy-start.3
  442.6 2.2 copy-start.1
  465.5 107.5 %all-to-all-start.1 = ((f32[64,64,256]{2,1,0:T(8,128)}), f32[64,64,256]{2,1,0:T(8,128)}, u32[]{:S(2)}, u32[]{:S(2)}) async-start(f32[64,64,256]{2,1,0:T(8,128)} %bitcast.206), calls=%async_computation.1 | async-start | bytes 8388608 | tf_op jit(solution)/shard_map/all_to_all | solution.py:112
Sparse Core Ops, SparseCore 0:
  229.0 41.9 all-reduce.6
  381.2 44.7 all-reduce.4
where the time goes:
time: 673 us; the launch traced here: 667 us
  local copies, waits for them, and re-layouts  292 us (43%)
  waiting for transfers between devices  233 us (35%)
  other arithmetic  49.8 us (7%)
  matrix products  44.1 us (7%)
  starting transfers between devices  26.1 us (4%)
  between operations  21.6 us (3%)
    all_to_all x1, waiting for transfers between devices, on_device(): lax.all_to_all(outgoing, 'blk', split_axis=1, concat_axis=0, tiled=True)  87.9 us
    psum x2, waiting for transfers between devices, summed_pair(): gram = lax.psum(local_gram(joined), 'row')  84.8 us
    scatter x3, local copies, waits for them, and re-layouts, inverse_of(): jnp.zeros(index.shape, jnp.int32).at[index]  63.5 us
    gather x1, local copies, waits for them, and re-layouts, on_device(): outgoing = jnp.take(flat, column_index(held, total_cols), axis=1)  58.2 us
    gather x1, local copies, waits for them, and re-layouts, on_device(): rotated = jnp.take(returned, inverse_of(placed), axis=1)  58.2 us
    all_to_all x1, waiting for transfers between devices, on_device(): lax.all_to_all(blocks, 'blk', split_axis=0, concat_axis=1, tiled=True)  35.8 us
    ppermute x2, waiting for transfers between devices, shifted(): return lax.ppermute(block, axis, route)  24.8 us
    gather x2, local copies, waits for them, and re-layouts, on_device(): blocks = jnp.take(joined, back, axis=1)  15.6 us
  transfers between devices with their start and end apart: 6, of which 6 were waited for; matrix products, arithmetic and copies ran while one was open for 11% of the time, Pallas kernels for 0%

commit v1 on v0

--- a/solution.py
+++ b/solution.py
@@ -2,6 +2,7 @@
 import jax.numpy as jnp
 from jax import lax
 from jax.sharding import PartitionSpec as P
+from jax.lax import all_to_all, axis_size
 
 ROWS = 16384
 BLOCK = 32
@@ -86,7 +87,9 @@
     held = assignment.reshape(nblk, SLOTS)
     flat = transmission.reshape(row_part, 2 * total_cols)
     outgoing = jnp.take(flat, column_index(held, total_cols), axis=1)
-    blocks = lax.all_to_all(outgoing, "blk", split_axis=1, concat_axis=0, tiled=True)
+    blocks = jnp.concatenate(
+        all_to_all(jnp.stack(jnp.split(outgoing, axis_size("blk"), axis=1), axis=0), "blk", 0, 0), 0
+    )
     owned_rows = blocks.shape[0]
     for rnd in range(ROUNDS):
         pick = pairing[rnd, me_blk]

time: 673 us -> 717 us (1.065)
  local copies, waits for them, and re-layouts: 292 us -> 333 us
    unnamed x15 -> x70, local copies, waits for them, and re-layouts: 8.42 us -> 50.2 us
    all_to_all x2 -> x0, local copies, waits for them, and re-layouts: 12.4 us -> none  [on_device(): lax.all_to_all(outgoing, 'blk', split_axis=1, concat_axis=0, tiled=True)]
    another operation x0 -> x2, local copies, waits for them, and re-layouts: none -> 7.48 us  [on_device(): jnp.stack(jnp.split(outgoing, axis_size('blk'), axis=1), axis=0)]
  transfers between devices with their start and end apart: 6 -> 6, of which waited for: 6 -> 6; matrix products, arithmetic and copies ran while one was open for 11% -> 10% of each run, Pallas kernels for 0% -> 0%
where the time goes in v1:
time: 717 us; the launch traced here: 710 us
  local copies, waits for them, and re-layouts  333 us (46%)
  waiting for transfers between devices  233 us (32%)
  other arithmetic  52.4 us (7%)
  matrix products  44 us (6%)
  starting transfers between devices  26 us (4%)
  between operations  21.5 us (3%)
    all_to_all x1, waiting for transfers between devices, on_device(): all_to_all(jnp.stack(jnp.split(outgoing, axis_size('blk'), axis=1), axis=...  88 us
    psum x2, waiting for transfers between devices, summed_pair(): gram = lax.psum(local_gram(joined), 'row')  84.6 us
    scatter x3, local copies, waits for them, and re-layouts, inverse_of(): jnp.zeros(index.shape, jnp.int32).at[index]  63.5 us
    gather x1, local copies, waits for them, and re-layouts, on_device(): outgoing = jnp.take(flat, column_index(held, total_cols), axis=1)  58.2 us
    gather x1, local copies, waits for them, and re-layouts, on_device(): rotated = jnp.take(returned, inverse_of(placed), axis=1)  58.2 us
    unnamed x70, local copies, waits for them, and re-layouts  50.2 us
    all_to_all x1, waiting for transfers between devices, on_device(): lax.all_to_all(blocks, 'blk', split_axis=0, concat_axis=1, tiled=True)  35.8 us
    ppermute x2, waiting for transfers between devices, shifted(): return lax.ppermute(block, axis, route)  24.8 us
  transfers between devices with their start and end apart: 6, of which 6 were waited for; matrix products, arithmetic and copies ran while one was open for 10% of the time, Pallas kernels for 0%

profile of v1, /device:TPU:6, one launch (start us, length us, event | category | flops | bytes accessed | tf_op | source)
XLA Modules:
  0.0 710.3 jit_solution(7517884165174291741)
XLA Ops:
  10.5 8.4 %copy.42 = f32[64,2,8192]{0,2,1:T(8,128)} copy(f32[64,2,8192]{2,1,0:T(2,128)} %param.14) | data formatting | bytes 8388608 | tf_op args[0]
  18.9 58.2 %gather_fusion = f32[16384,64]{1,0:T(8,128)} fusion(f32[64,16384]{0,1:T(8,128)} %bitcast.456, s32[16384]{0:T(1024)S(1)} %fusion.68), kind=kCustom, calls=%fused_computation.clone | custom fusion | bytes 8454144 | tf_op jit(solution)/shard_map/jit(_take)/gather | solution.py:89
  77.0 11.8 %select_bitcast_fusion = f32[64,16384]{0,1:T(8,128)S(1)} fusion(f32[16384,64]{1,0:T(8,128)} %gather_fusion, pred[16384]{0:T(1024)(128)(4,1)S(1)} %compare_and_fusion.1), kind=kLoop, calls=%fused_computation.15 | loop fusion | flops 1048576 | bytes 8404992 | tf_op jit(solution)/shard_map/jit(_take)/select_n | solution.py:89
  131.3 6.8 copy.43
  138.1 13.2 %all-to-all-start = ((f32[64,64,256]{2,1,0:T(8,128)}), f32[64,64,256]{2,1,0:T(8,128)}, u32[]{:S(2)}, u32[]{:S(2)}) async-start(f32[64,64,256]{2,1,0:T(8,128)} %copy.43), calls=%async_computation | async-start | bytes 8388608 | tf_op jit(solution)/shard_map/all_to_all | solution.py:91
  158.8 88.0 %all-to-all-done = f32[64,64,256]{2,1,0:T(8,128)} async-done(((f32[64,64,256]{2,1,0:T(8,128)}), f32[64,64,256]{2,1,0:T(8,128)}, u32[]{:S(2)}, u32[]{:S(2)}) %all-to-all-start) | async-done | bytes 4194336 | tf_op jit(solution)/shard_map/all_to_all | solution.py:91
  246.8 5.6 copy.44
  252.4 5.6 gather_fusion.1
  272.2 40.0 %all-reduce.7.cloned.1.call-done = (f32[128,128]{1,0:T(8,128)}, f32[128,128]{1,0:T(8,128)}) async-done(((f32[128,128]{1,0:T(8,128)}, f32[128,128]{1,0:T(8,128)}), (f32[128,128]{1,0:T(8,128)}, f32[128,128]{1,0:T(8,128)})) %all-reduce.7.cloned.1.call-update) | async-done | bytes 131088 | tf_op jit(solution)/shard_map/psum | solution.py:51
  335.6 7.8 %gather_fusion.3 = f32[256,4096]{1,0:T(8,128)} fusion(f32[4096,256]{0,1:T(8,128)} %pad_maximum_fusion, s32[1024]{0:T(1024)S(1)} %pad_clamp_fusion.5), kind=kCustom, calls=%fused_computation.2.clone | custom fusion | bytes 8389632 | tf_op jit(solution)/shard_map/jit(_take)/gather | solution.py:105
  362.0 17.9 %collective-permute-done = f32[2048,128]{1,0:T(8,128)} collective-permute-done((f32[2048,128]{1,0:T(8,128)}, f32[2048,128]{1,0:T(8,128)}, u32[]{:S(2)}, u32[]{:S(2)}) %collective-permute-start) | collective-permute-done | bytes 1048608 | tf_op jit(solution)/shard_map/ppermute | solution.py:17
  382.1 6.9 collective-permute-done.1
  399.2 5.5 scatter_fusion.1
  404.7 5.7 gather_fusion.6
  422.4 44.6 %all-reduce.5.cloned.1.call-done = (f32[128,128]{1,0:T(8,128)}, f32[128,128]{1,0:T(8,128)}) async-done(((f32[128,128]{1,0:T(8,128)}, f32[128,128]{1,0:T(8,128)}), (f32[128,128]{1,0:T(8,128)}, f32[128,128]{1,0:T(8,128)})) %all-reduce.5.cloned.1.call-update) | async-done | bytes 131088 | tf_op jit(solution)/shard_map/psum | solution.py:51
  490.7 7.8 %gather_fusion.8 = f32[256,4096]{1,0:T(8,128)} fusion(f32[4096,256]{0,1:T(8,128)} %pad_maximum_fusion.1, s32[1024]{0:T(1024)S(1)} %pad_clamp_fusion), kind=kCustom, calls=%fused_computation.8.clone | custom fusion | bytes 8389632 | tf_op jit(solution)/shard_map/jit(_take)/gather | solution.py:105
  503.3 5.6 copy.50
  508.9 10.7 %all-to-all-start.1 = ((f32[64,64,256]{2,1,0:T(8,128)}), f32[64,64,256]{2,1,0:T(8,128)}, u32[]{:S(2)}, u32[]{:S(2)}) async-start(f32[64,64,256]{2,1,0:T(8,128)} %bitcast.458), calls=%async_computation.1 | async-start | bytes 8388608 | tf_op jit(solution)/shard_map/all_to_all | solution.py:115
  520.2 60.3 %scatter_custom_fusion.4 = s32[16384]{0:T(1024)S(1)} fusion(s32[16384]{0:T(1024)S(1)} %bitcast.461, s32[16384]{0:T(1024)S(1)} %iota.215, s32[]{:T(128)} %constant.15.clone.1), kind=kCustom, calls=%fused_computation.280 | custom fusion | bytes 65540 | tf_op jit(solution)/shard_map/scatter | solution.py:71
  580.6 35.8 %all-to-all-done.1 = f32[64,64,256]{2,1,0:T(8,128)} async-done(((f32[64,64,256]{2,1,0:T(8,128)}), f32[64,64,256]{2,1,0:T(8,128)}, u32[]{:S(2)}, u32[]{:S(2)}) %all-to-all-start.1) | async-done | bytes 4194336 | tf_op jit(solution)/shard_map/all_to_all | solution.py:115
  616.4 6.9 copy.51
  623.3 58.2 %gather_fusion.9 = f32[16384,64]{1,0:T(8,128)} fusion(f32[64,16384]{0,1:T(8,128)} %bitcast.455, s32[16384]{0:T(1024)S(1)} %fusion.69), kind=kCustom, calls=%fused_computation.4.clone | custom fusion | bytes 8454144 | tf_op jit(solution)/shard_map/jit(_take)/gather | solution.py:117
  681.5 13.1 %broadcast_select_fusion = f32[16384,64]{1,0:T(8,128)} fusion(f32[16384,64]{1,0:T(8,128)} %gather_fusion.9, pred[16384]{0:T(1024)(128)(4,1)S(1)} %compare_and_fusion), kind=kLoop, calls=%fused_computation.20 | loop fusion | flops 1048576 | bytes 8404992 | tf_op jit(solution)/shard_map/jit(_take)/select_n | solution.py:117
  694.6 8.6 %copy.52 = f32[64,2,8192]{2,1,0:T(2,128)} copy(f32[64,2,8192]{0,2,1:T(8,128)} %bitcast.457) | data formatting | bytes 8388608 | tf_op jit(solution)/shard_map/reshape | solution.py:118
  (255 shorter events, 155.8 us)
Async XLA Ops:
  131.3 20.0 %copy-start = (s32[2,64]{1,0:T(2,128)S(1)}, s32[2,64]{1,0:T(2,128)}, u32[]{:S(2)}) copy-start(s32[2,64]{1,0:T(2,128)} %param.16) | copy-start | bytes 1540
  131.3 24.3 %copy-start.1 = (s32[3,4]{1,0:T(4,128)S(1)}, s32[3,4]{1,0:T(4,128)}, u32[]{:S(2)}) copy-start(s32[3,4]{1,0:T(4,128)} %constant.22.clone) | copy-start | bytes 148
  138.1 108.7 %all-to-all-start = ((f32[64,64,256]{2,1,0:T(8,128)}), f32[64,64,256]{2,1,0:T(8,128)}, u32[]{:S(2)}, u32[]{:S(2)}) async-start(f32[64,64,256]{2,1,0:T(8,128)} %copy.43), calls=%async_computation | async-start | bytes 8388608 | tf_op jit(solution)/shard_map/all_to_all | solution.py:91
  151.3 160.9 %all-reduce.7.cloned.1.call-start = ((), (), s32[]{:S(2)}) async-start(), calls=%async_computation.3 | async-start | bytes 262144 | tf_op jit(solution)/shard_map/psum | solution.py:51
  270.0 197.0 %all-reduce.5.cloned.1.call-start = ((), (), s32[]{:S(2)}) async-start(), calls=%async_computation.2 | async-start | bytes 262144 | tf_op jit(solution)/shard_map/psum | solution.py:51
  354.2 25.7 %collective-permute-start = (f32[2048,128]{1,0:T(8,128)}, f32[2048,128]{1,0:T(8,128)}, u32[]{:S(2)}, u32[]{:S(2)}) collective-permute-start(f32[2048,128]{1,0:T(8,128)} %reshape.610), channel_id=1, source_target_pairs={{252,0},{0,4},{4,8},{8,12},{12,16},{16,20},{20,24},{24,28},{28,32}... | collective-permute-start | bytes 3145736 | tf_op jit(solution)/shard_map/ppermute | solution.py:17
  361.4 27.5 %collective-permute-start.1 = (f32[2048,128]{1,0:T(8,128)}, f32[2048,128]{1,0:T(8,128)}, u32[]{:S(2)}, u32[]{:S(2)}) collective-permute-start(f32[2048,128]{1,0:T(8,128)} %reshape.612), channel_id=1, source_target_pairs={{4,0},{8,4},{12,8},{16,12},{20,16},{24,20},{28,24},{32,28},{36,32}... | collective-permute-start | bytes 3145736 | tf_op jit(solution)/shard_map/ppermute | solution.py:17
  508.9 107.5 %all-to-all-start.1 = ((f32[64,64,256]{2,1,0:T(8,128)}), f32[64,64,256]{2,1,0:T(8,128)}, u32[]{:S(2)}, u32[]{:S(2)}) async-start(f32[64,64,256]{2,1,0:T(8,128)} %bitcast.458), calls=%async_computation.1 | async-start | bytes 8388608 | tf_op jit(solution)/shard_map/all_to_all | solution.py:115
Sparse Core Ops, SparseCore 0:
  270.2 41.9 all-reduce.6
  422.5 44.5 all-reduce.4
